TPU v7x, 256 devices: a whole 4x4x8 slice. The times are simulated.
256 devices in a mesh: space: 8 (over y, x_hi), group: 32 (over z, x_lo, core).
Axes of the slice: x: 4 (x_hi: 2, x_lo: 2; x = x_hi * 2 + x_lo), y: 4, z: 8, core: 2. Of those that a mesh axis runs over, the one named last changes fastest.
Arguments:
- perturbations: float32 [32, 4, 32, 64, 256], P('group', None, 'space'), may hold values from -6 to 6
- trajectory: bfloat16 [32, 8, 32, 64, 256], P('group', None, 'space'), may hold values from -0.25 to 0.25
- slot_table: int32 [32], replicated, may hold values from 0 to 31, each once
- step_indices: int32 [2], replicated, may hold values from 0 to 31
Outputs:
- evolved: float32 [32, 4, 32, 64, 256], P('group', None, 'space')
Inputs may be any that keep to these rules, and one draw needn't show every extreme that they name: `slot_table`: each storage row appears exactly once.
All inputs are finite; a program needn't handle non-finite values.
Results may differ from a plain program's by a relative error of at most 0.00089.
Values may be sent and summed in bfloat16 or wider, within the bound.
No kernel may reach another device: no remote copies, remote signals or barrier semaphores. Data moves between devices by JAX's collectives and lax.ppermute only.
A program may use at most 64 MiB of HBM per device.

v0:
```python
import functools

import jax
import jax.numpy as jnp
from jax import lax
from jax.experimental import pallas as pl
from jax.experimental.pallas import tpu as pltpu
from jax.sharding import PartitionSpec as P

STEPS = 2

SATURATION_SLOPE = 2.0
SHARPNESS = 4.0
CONDENSE_RATE = 0.25
LATENT_HEAT = 0.3

GROUP = 32
RING = 8


def spot(z, x, c):
    return (z % RING) * 4 + x * 2 + c


def shift_pattern(step, planes=range(RING)):
    return [
        (spot(z, x, c), spot(z + step, x, c)) for z in planes for x in range(2) for c in range(2)
    ]


X_PATTERN = [(i, i ^ 2) for i in range(GROUP)]
C_PATTERN = [(i, i ^ 1) for i in range(GROUP)]


def move(value, pattern):
    return lax.ppermute(value, "group", pattern)


def decode_kernel(
    stored_hbm, table_hbm, steps_hbm, fields_hbm,
    keep_ref, send_ref, first_ref, last_ref, owner_ref,
    stored_ref, table_ref, steps_ref, edge_ref, sems,
):
    small = [
        pltpu.make_async_copy(table_hbm, table_ref, sems.at[4]),
        pltpu.make_async_copy(steps_hbm, steps_ref, sems.at[5]),
    ]
    copies = [
        pltpu.make_async_copy(stored_hbm.at[0, :, p], stored_ref.at[p], sems.at[p]) for p in range(4)
    ]
    sides = [
        pltpu.make_async_copy(fields_hbm.at[0, :, 3 * k], edge_ref.at[k], sems.at[6 + k])
        for k in range(2)
    ]
    for copy in small + copies + sides:
        copy.start()
    first = lax.rem(lax.axis_index("group"), 2) == 0
    for p in range(4):
        copies[p].wait()
        for start in range(0, 64, 32):
            rows = slice(start, start + 32)
            potential, exner_value, moisture, density = (
                1.0 + scale * stored_ref[p, k, rows, :].astype(jnp.float32)
                for k, scale in ((4, 0.4), (5, 0.4), (6, 2.0), (7, 0.8))
            )
            saturated = jnp.exp(SATURATION_SLOPE * (potential * exner_value - 1.0)) / density
            weight = jax.nn.sigmoid(SHARPNESS * (moisture - saturated))
            uptake = weight.astype(jnp.bfloat16)
            coupling = (weight * SATURATION_SLOPE * exner_value * saturated).astype(jnp.bfloat16)
            low = [stored_ref[p, k, rows, :] for k in range(3)]
            high = [stored_ref[p, 3, rows, :], uptake, coupling]
            for k in range(3):
                keep_ref[4 * k + p, rows, :] = jnp.where(first, low[k], high[k])
                send_ref[4 * k + p, rows, :] = jnp.where(first, high[k], low[k])
    for k, target in enumerate((first_ref, last_ref)):
        sides[k].wait()
        target[...] = edge_ref[k].astype(jnp.bfloat16)
    for copy in small:
        copy.wait()
    owner_ref[0] = table_ref[steps_ref[0]] + GROUP * table_ref[steps_ref[1]]


def decode_slice(trajectory, slot_table, step_indices, perturbations):
    vmem = pl.BlockSpec(memory_space=pltpu.VMEM)
    half = jax.ShapeDtypeStruct((12, 64, 256), jnp.bfloat16)
    edge = jax.ShapeDtypeStruct((4, 64, 256), jnp.bfloat16)
    return pl.pallas_call(
        decode_kernel,
        out_shape=(half, half, edge, edge, jax.ShapeDtypeStruct((1,), jnp.int32)),
        in_specs=[pl.BlockSpec(memory_space=pltpu.HBM)] * 4,
        out_specs=(vmem, vmem, vmem, vmem, pl.BlockSpec(memory_space=pltpu.SMEM)),
        scratch_shapes=[
            pltpu.VMEM((4, 8, 64, 256), jnp.bfloat16),
            pltpu.SMEM((GROUP,), jnp.int32),
            pltpu.SMEM((STEPS,), jnp.int32),
            pltpu.VMEM((2, 4, 64, 256), jnp.float32),
            pltpu.SemaphoreType.DMA((8,)),
        ],
        compiler_params=pltpu.CompilerParams(vmem_limit_bytes=56 * 1024 * 1024),
        cost_estimate=pl.CostEstimate(
            flops=1_500_000, bytes_accessed=2_800_000, transcendentals=200_000
        ),
    )(trajectory, slot_table, step_indices, perturbations)


def step_kernel(edge_ref, q_ref, low_ref, high_ref, coef_ref, out_ref):
    planes, levels, width = q_ref.shape[1:]
    block = 16
    low_on, high_on = edge_ref[0], edge_ref[1]
    column = lax.broadcasted_iota(jnp.int32, (block, width), 1)
    row = lax.broadcasted_iota(jnp.int32, (block, width), 0)

    for plane in range(planes):
        for start in range(0, levels, block):
            rows = slice(start, start + block)
            speed = [coef_ref[k, plane, rows, :].astype(jnp.float32) for k in range(6)]
            diffusion = 0.025 + 0.06 * speed[3]
            west_w = jnp.maximum(speed[0], 0.0) + diffusion
            east_w = diffusion - jnp.minimum(speed[0], 0.0)
            south_w = jnp.maximum(speed[1], 0.0) + diffusion
            north_w = diffusion - jnp.minimum(speed[1], 0.0)
            below_w = jnp.maximum(speed[2], 0.0) + diffusion
            above_w = diffusion - jnp.minimum(speed[2], 0.0)
            centre_w = 1.0 - (west_w + east_w + south_w + north_w + below_w + above_w)
            south_w = jnp.where(column == 0, 0.0, south_w)
            north_w = jnp.where(column == width - 1, 0.0, north_w)
            if start == 0:
                below_w = jnp.where(row == 0, 0.0, below_w)
            if start + block == levels:
                above_w = jnp.where(row == block - 1, 0.0, above_w)
            if plane == 0:
                west_w = west_w * low_on
            if plane == planes - 1:
                east_w = east_w * high_on
            carried = []
            for field in range(4):
                centre = q_ref[field, plane, rows, :]
                if plane == 0:
                    west = low_ref[field, rows, :].astype(jnp.float32)
                else:
                    west = q_ref[field, plane - 1, rows, :]
                if plane == planes - 1:
                    east = high_ref[field, rows, :].astype(jnp.float32)
                else:
                    east = q_ref[field, plane + 1, rows, :]
                south = pltpu.roll(centre, 1, 1)
                north = pltpu.roll(centre, width - 1, 1)
                if start == 0:
                    below = pltpu.roll(centre, 1, 0)
                else:
                    below = q_ref[field, plane, start - 1 : start + block - 1, :]
                if start + block == levels:
                    above = pltpu.roll(centre, block - 1, 0)
                else:
                    above = q_ref[field, plane, start + 1 : start + block + 1, :]
                carried.append(
                    (centre_w * centre + west_w * west)
                    + (east_w * east + south_w * south)
                    + (north_w * north + below_w * below)
                    + above_w * above
                )
            condense = CONDENSE_RATE * (speed[4] * carried[1] - speed[5] * carried[0])
            out_ref[0, plane, rows, :] = carried[0] + LATENT_HEAT * condense
            out_ref[1, plane, rows, :] = carried[1] - condense
            out_ref[2, plane, rows, :] = carried[2] + condense
            out_ref[3, plane, rows, :] = carried[3]


def advance(fields, low, high, coefficients, edges):
    vmem = pl.BlockSpec(memory_space=pltpu.VMEM)
    return pl.pallas_call(
        step_kernel,
        out_shape=jax.ShapeDtypeStruct(fields.shape, jnp.float32),
        in_specs=[pl.BlockSpec(memory_space=pltpu.SMEM), vmem, vmem, vmem, vmem],
        out_specs=vmem,
        compiler_params=pltpu.CompilerParams(vmem_limit_bytes=24 * 1024 * 1024),
        cost_estimate=pl.CostEstimate(
            flops=8_000_000, bytes_accessed=4_000_000, transcendentals=0
        ),
    )(edges, fields, low, high, coefficients)


def ring_patterns():
    count = lax.axis_size("space")
    forward = [(i, (i + 1) % count) for i in range(count)]
    return forward, [(target, source) for source, target in forward]


def ring_halo(first, last):
    forward, backward = ring_patterns()
    return lax.ppermute(last, "space", forward), lax.ppermute(first, "space", backward)


def pick(flag, yes, no):
    return jnp.where(flag, yes, no)


def far_branch(plane):
    def send(piece):
        return move(piece, shift_pattern(3, [plane])), move(piece, shift_pattern(-3, [plane]))

    return send


def far(piece, plane, distance):
    up, down = lax.switch(plane, [far_branch(p) for p in range(RING)], piece)
    return pick(distance == 3, up, pick(distance == 5, down, piece))


def near(held, distance):
    plus = move(held, shift_pattern(1))
    minus = move(held, shift_pattern(-1))
    keep = (distance == 0) | (distance == 3) | (distance == 5)
    from_low = (distance == 1) | (distance == 4) | (distance == 6)
    return pick(keep, held, pick(from_low, plus, minus))


def on_device(perturbations, trajectory, slot_table, step_indices):
    fields = perturbations[0]
    me = lax.axis_index("group")
    my_z, my_x, my_c = me // 4, (me // 2) % 2, me % 2
    space = lax.axis_index("space")
    edges = jnp.stack([space > 0, space < lax.axis_size("space") - 1]).astype(jnp.float32)

    mine, sent, first, last, packed = decode_slice(
        trajectory, slot_table, step_indices, perturbations
    )
    other = move(sent, C_PATTERN)
    packed = packed[0]
    owners = [packed % GROUP, packed // GROUP]
    planes = [owner // 4 for owner in owners]
    distance = [(my_z - z) % RING for z in planes]
    low, high = ring_halo(first, last)

    pieces = []
    for k, owner in enumerate(owners):
        half = pick(owner % 2 == my_c, mine, other).reshape(2, 6, 64, 256)
        keep = lax.dynamic_index_in_dim(half, my_x, 0, keepdims=False)
        got = move(lax.dynamic_index_in_dim(half, 1 - my_x, 0, keepdims=False), X_PATTERN)
        pieces.append(pick((owner // 2) % 2 == my_x, keep, got))
    pieces[1], low, high = lax.optimization_barrier((pieces[1], low, high))
    pieces = [
        near(far(piece, z, d), d) for piece, z, d in zip(pieces, planes, distance)
    ]

    for k in range(STEPS):
        piece = pieces[k]
        got = move(piece, X_PATTERN)
        half = jnp.concatenate(
            [pick(my_x == 0, piece, got), pick(my_x == 0, got, piece)], axis=0
        )
        got = move(half, C_PATTERN)
        whole = jnp.concatenate(
            [pick(my_c == 0, half, got), pick(my_c == 0, got, half)], axis=0
        ).reshape(6, 4, 64, 256)
        fields = advance(fields, low, high, whole, edges)
        if k + 1 < STEPS:
            low, high = ring_halo(
                fields[:, 0].astype(jnp.bfloat16), fields[:, -1].astype(jnp.bfloat16)
            )
    return fields[None]


def solution(mesh):
    return jax.shard_map(
        on_device,
        mesh=mesh,
        in_specs=(
            P("group", None, "space", None, None),
            P("group", None, "space", None, None),
            P(),
            P(),
        ),
        out_specs=P("group", None, "space", None, None),
        check_vma=False,
    )
```

profile of v0, /device:TPU:1, one launch (start us, length us, event | category | flops | bytes accessed | tf_op | source)
XLA Modules:
  0.0 76.8 jit_solution(5157958844482750563)
XLA Ops:
  0.0 2.4 %shard_map.46 = (bf16[12,64,256]{2,1,0:T(8,128)(2,1)}, bf16[12,64,256]{2,1,0:T(8,128)(2,1)}, bf16[4,64,256]{2,1,0:T(8,128)(2,1)}, bf16[4,64,256]{2,1,0:T(8,128)(2,1)}, s32[1]{0:T(128)}) custom-call(bf16[1,8,4,64,256]{4,3,2,1,0:T(8,128)(2,1)} %stored_hbm.1, s32[32]{0:T(128)} %table_hbm.1, s32[2]{0:T(128)} %steps_hbm.1, f32[1,4,4,64,256]{4,3,2,1,0:T(8,128)} %fields_hbm.1), custom_call_target="tpu_custom_call" | custom-call | flops 1500000 | bytes 2800000 | tf_op jit(solution)/shard_map/pallas_call | solution.py:87
  2.4 3.3 %collective-permute-start.32 = (bf16[12,64,256]{2,1,0:T(8,128)(2,1)}, bf16[12,64,256]{2,1,0:T(8,128)(2,1)S(1)}, u32[]{:S(2)}, u32[]{:S(2)}) collective-permute-start(bf16[12,64,256]{2,1,0:T(8,128)(2,1)} %get-tuple-element.35), channel_id=1, source_target_pairs={{0,1},{1,0},{2,3},{3,2},{4,5},{5,4},{6,7},{7,6},{8,9},{9,8},{10,11... | collective-permute-start | bytes 1179656 | tf_op jit(solution)/shard_map/ppermute | solution.py:36
  8.3 0.0 collective-permute-done.32
  8.4 1.1 %broadcast_select_fusion = (bf16[12,64,256]{2,1,0:T(8,128)(2,1)S(1)}, bf16[12,64,256]{2,1,0:T(8,128)(2,1)S(1)}) fusion(bf16[12,64,256]{2,1,0:T(8,128)(2,1)} %get-tuple-element.34, bf16[12,64,256]{2,1,0:T(8,128)(2,1)S(1)} %collective-permute-done.32, pred[]{:T(512)S(6)} %eq.82, pred[]{:T(512)S(6)} %eq.75), kind=kLoop, calls=%fused_computation.5 | loop fusion | flops 393216 | bytes 1572866 | tf_op jit(solution)/shard_map/jit(_where)/select_n | solution.py:195
  9.4 0.0 copy-start.2
  9.4 0.0 copy-start.1
  9.5 0.1 collective-permute-start.36
  9.6 0.8 copy-done.2
  10.3 1.2 %collective-permute-start.34 = (bf16[4,64,256]{2,1,0:T(8,128)(2,1)S(1)}, bf16[4,64,256]{2,1,0:T(8,128)(2,1)S(1)}, u32[]{:S(2)}, u32[]{:S(2)}) collective-permute-start(bf16[4,64,256]{2,1,0:T(8,128)(2,1)S(1)} %copy-done.2), channel_id=1, source_target_pairs={{0,32},{32,64},{64,96},{96,128},{128,160},{160,192},{192,224},{224... | collective-permute-start | bytes 393224 | tf_op jit(solution)/shard_map/ppermute | solution.py:191
  11.5 0.0 copy-done.1
  11.5 3.9 %collective-permute-start.35 = (bf16[4,64,256]{2,1,0:T(8,128)(2,1)S(1)}, bf16[4,64,256]{2,1,0:T(8,128)(2,1)S(1)}, u32[]{:S(2)}, u32[]{:S(2)}) collective-permute-start(bf16[4,64,256]{2,1,0:T(8,128)(2,1)S(1)} %copy-done.1), channel_id=1, source_target_pairs={{32,0},{64,32},{96,64},{128,96},{160,128},{192,160},{224,192},{0,2... | collective-permute-start | bytes 393224 | tf_op jit(solution)/shard_map/ppermute | solution.py:191
  15.4 0.8 %collective-permute-start.33 = (bf16[6,64,256]{2,1,0:T(8,128)(2,1)S(1)}, bf16[6,64,256]{2,1,0:T(8,128)(2,1)S(1)}, u32[]{:S(2)}, u32[]{:S(2)}) collective-permute-start(bf16[6,64,256]{2,1,0:T(8,128)(2,1)S(1)} %dynamic-slice_bitcast_fusion.1), channel_id=1, source_target_pairs={{0,2},{1,3},{2,0},{3,1},{4,6},{5,7},{6,4},{7,5},{8,10},{9,11},{10,... | collective-permute-start | bytes 589832 | tf_op jit(solution)/shard_map/ppermute | solution.py:36
  16.2 0.0 collective-permute-done.36
  16.2 2.7 %conditional.2 = (bf16[6,64,256]{2,1,0:T(8,128)(2,1)}, bf16[6,64,256]{2,1,0:T(8,128)(2,1)}) conditional(s32[]{:T(128)} %clamp.6, bf16[6,64,256]{2,1,0:T(8,128)(2,1)S(1)} %bitcast_select_fusion, bf16[6,64,256]{2,1,0:T(8,128)(2,1)S(1)} %bitcast_select_fusion, bf16[6,64,256]{2,1,0:T(8,128)(2,1)S(1)} %bitcast_select_fusion, ...), branch_computations={%region_0.1_spmd, %region_1.2_spmd, %region_2.3_spmd, %region_3.4_... | conditional | bytes 1572960 | solution.py:206
  16.3 1.3 %collective-permute-start.9 = (bf16[6,64,256]{2,1,0:T(8,128)(2,1)S(1)}, bf16[6,64,256]{2,1,0:T(8,128)(2,1)}, u32[]{:S(2)}, u32[]{:S(2)}) collective-permute-start(bf16[6,64,256]{2,1,0:T(8,128)(2,1)S(1)} %param.4), channel_id=1, source_target_pairs={{16,4},{17,5},{18,6},{19,7},{48,36},{49,37},{50,38},{51,39},{80,68... | collective-permute-start | bytes 589832 | tf_op jit(solution)/shard_map/cond/branch_4_fun/ppermute | solution.py:36
  17.6 1.3 %collective-permute-start.8 = (bf16[6,64,256]{2,1,0:T(8,128)(2,1)S(1)}, bf16[6,64,256]{2,1,0:T(8,128)(2,1)}, u32[]{:S(2)}, u32[]{:S(2)}) collective-permute-start(bf16[6,64,256]{2,1,0:T(8,128)(2,1)S(1)} %param.4), channel_id=1, source_target_pairs={{16,28},{17,29},{18,30},{19,31},{48,60},{49,61},{50,62},{51,63},{8... | collective-permute-start | bytes 589832 | tf_op jit(solution)/shard_map/cond/branch_4_fun/ppermute | solution.py:36
  18.9 0.0 collective-permute-done.9
  18.9 0.0 collective-permute-done.8
  19.0 13.3 %collective-permute-start.38 = (bf16[6,64,256]{2,1,0:T(8,128)(2,1)S(1)}, bf16[6,64,256]{2,1,0:T(8,128)(2,1)S(1)}, u32[]{:S(2)}, u32[]{:S(2)}) collective-permute-start(bf16[6,64,256]{2,1,0:T(8,128)(2,1)S(1)} %select_select_fusion.3), channel_id=1, source_target_pairs={{0,28},{1,29},{2,30},{3,31},{4,0},{5,1},{6,2},{7,3},{8,4},{9,5},{1... | collective-permute-start | bytes 589832 | tf_op jit(solution)/shard_map/ppermute | solution.py:36
  32.3 0.0 collective-permute-start.37
  32.3 0.0 collective-permute-done.33
  32.4 0.0 collective-permute-done.34.low_ref
  32.4 0.0 collective-permute-done.35.high_ref
  32.4 2.7 %conditional.3 = (bf16[6,64,256]{2,1,0:T(8,128)(2,1)}, bf16[6,64,256]{2,1,0:T(8,128)(2,1)}) conditional(s32[]{:T(128)} %clamp.7, bf16[6,64,256]{2,1,0:T(8,128)(2,1)S(1)} %bitcast_select_fusion.1, bf16[6,64,256]{2,1,0:T(8,128)(2,1)S(1)} %bitcast_select_fusion.1, ...), branch_computations={%region_8.9_spmd, %region_9.10_spmd, %region_10.11_spmd, %region_1... | conditional | bytes 1572960 | solution.py:206
  32.4 1.3 %collective-permute-start.31 = (bf16[6,64,256]{2,1,0:T(8,128)(2,1)S(1)}, bf16[6,64,256]{2,1,0:T(8,128)(2,1)}, u32[]{:S(2)}, u32[]{:S(2)}) collective-permute-start(bf16[6,64,256]{2,1,0:T(8,128)(2,1)S(1)} %param.15), channel_id=1, source_target_pairs={{28,16},{29,17},{30,18},{31,19},{60,48},{61,49},{62,50},{63,51},{9... | collective-permute-start | bytes 589832 | tf_op jit(solution)/shard_map/cond/branch_7_fun/ppermute | solution.py:36
  33.7 1.3 %collective-permute-start.30 = (bf16[6,64,256]{2,1,0:T(8,128)(2,1)S(1)}, bf16[6,64,256]{2,1,0:T(8,128)(2,1)}, u32[]{:S(2)}, u32[]{:S(2)}) collective-permute-start(bf16[6,64,256]{2,1,0:T(8,128)(2,1)S(1)} %param.15), channel_id=1, source_target_pairs={{28,8},{29,9},{30,10},{31,11},{60,40},{61,41},{62,42},{63,43},{92,... | collective-permute-start | bytes 589832 | tf_op jit(solution)/shard_map/cond/branch_7_fun/ppermute | solution.py:36
  35.1 0.0 collective-permute-done.31
  35.1 0.0 collective-permute-done.30
  35.1 8.0 %collective-permute-start.44 = (bf16[6,64,256]{2,1,0:T(8,128)(2,1)S(1)}, bf16[6,64,256]{2,1,0:T(8,128)(2,1)S(1)}, u32[]{:S(2)}, u32[]{:S(2)}) collective-permute-start(bf16[6,64,256]{2,1,0:T(8,128)(2,1)S(1)} %select_select_fusion.1), channel_id=1, source_target_pairs={{0,28},{1,29},{2,30},{3,31},{4,0},{5,1},{6,2},{7,3},{8,4},{9,5},{1... | collective-permute-start | bytes 589832 | tf_op jit(solution)/shard_map/ppermute | solution.py:36
  43.1 0.0 collective-permute-start.43
  43.1 0.0 collective-permute-done.38
  43.1 0.0 collective-permute-done.37
  43.2 0.4 collective-permute-start.39
  43.6 2.1 %collective-permute-done.44 = bf16[6,64,256]{2,1,0:T(8,128)(2,1)S(1)} collective-permute-done((bf16[6,64,256]{2,1,0:T(8,128)(2,1)S(1)}, bf16[6,64,256]{2,1,0:T(8,128)(2,1)S(1)}, u32[]{:S(2)}, u32[]{:S(2)}) %collective-permute-start.44) | collective-permute-done | bytes 196640 | tf_op jit(solution)/shard_map/ppermute | solution.py:36
  45.7 3.1 %collective-permute-done.43 = bf16[6,64,256]{2,1,0:T(8,128)(2,1)S(1)} collective-permute-done((bf16[6,64,256]{2,1,0:T(8,128)(2,1)S(1)}, bf16[6,64,256]{2,1,0:T(8,128)(2,1)S(1)}, u32[]{:S(2)}, u32[]{:S(2)}) %collective-permute-start.43) | collective-permute-done | bytes 196640 | tf_op jit(solution)/shard_map/ppermute | solution.py:36
  48.9 0.4 collective-permute-start.45
  49.3 0.0 collective-permute-done.39
  49.4 4.0 %collective-permute-start.40 = (bf16[12,64,256]{2,1,0:T(8,128)(2,1)S(1)}, bf16[12,64,256]{2,1,0:T(8,128)(2,1)S(1)}, u32[]{:S(2)}, u32[]{:S(2)}) collective-permute-start(bf16[12,64,256]{2,1,0:T(8,128)(2,1)S(1)} %pad_maximum_fusion.2), channel_id=1, source_target_pairs={{0,1},{1,0},{2,3},{3,2},{4,5},{5,4},{6,7},{7,6},{8,9},{9,8},{10,11... | collective-permute-start | bytes 1179656 | tf_op jit(solution)/shard_map/ppermute | solution.py:36
  53.4 0.1 add_convert_fusion.edge_ref
  53.4 0.0 collective-permute-done.45
  53.6 4.6 %collective-permute-start.46 = (bf16[12,64,256]{2,1,0:T(8,128)(2,1)S(1)}, bf16[12,64,256]{2,1,0:T(8,128)(2,1)S(1)}, u32[]{:S(2)}, u32[]{:S(2)}) collective-permute-start(bf16[12,64,256]{2,1,0:T(8,128)(2,1)S(1)} %pad_maximum_fusion.3), channel_id=1, source_target_pairs={{0,1},{1,0},{2,3},{3,2},{4,5},{5,4},{6,7},{7,6},{8,9},{9,8},{10,11... | collective-permute-start | bytes 1179656 | tf_op jit(solution)/shard_map/ppermute | solution.py:36
  58.2 0.0 collective-permute-done.40
  58.2 0.1 broadcast_select_fusion.4
  58.3 0.0 copy-start
  58.3 0.1 pad_maximum_fusion
  58.4 1.1 %copy-done = f32[1,4,4,64,256]{4,3,2,1,0:T(8,128)S(1)} copy-done((f32[1,4,4,64,256]{4,3,2,1,0:T(8,128)S(1)}, f32[1,4,4,64,256]{4,3,2,1,0:T(8,128)}, u32[]{:S(2)}) %copy-start) | copy-done | bytes 1048600
  59.5 1.6 %shard_map.47.q_ref = f32[4,4,64,256]{3,2,1,0:T(8,128)S(1)} custom-call(f32[2]{0:T(128)S(1)} %add_convert_fusion.edge_ref, f32[4,4,64,256]{3,2,1,0:T(8,128)S(1)} %bitcast.21, bf16[4,64,256]{2,1,0:T(8,128)(2,1)S(1)} %collective-permute-done.34.low_ref, bf16[4,64,256]{2,1,0:T(8,128)(2,1)S(1)} %collective-permute-done.35.high_ref, ...), custom_call_target="tpu_custom_call" | custom-call | flops 8000000 | bytes 4000000 | tf_op jit(solution)/shard_map/pallas_call | solution.py:171
  61.1 4.6 %collective-permute-start.42 = (bf16[4,64,256]{2,1,0:T(8,128)(2,1)S(1)}, bf16[4,64,256]{2,1,0:T(8,128)(2,1)S(1)}, u32[]{:S(2)}, u32[]{:S(2)}) collective-permute-start(bf16[4,64,256]{2,1,0:T(8,128)(2,1)S(1)} %get-tuple-element.51), channel_id=1, source_target_pairs={{32,0},{64,32},{96,64},{128,96},{160,128},{192,160},{224,192},{0,2... | collective-permute-start | bytes 393224 | tf_op jit(solution)/shard_map/ppermute | solution.py:191
  65.8 0.0 collective-permute-start.41
  65.8 0.0 collective-permute-done.46
  65.8 0.1 broadcast_select_fusion.2
  65.9 0.1 pad_maximum_fusion.1
  65.9 2.8 %collective-permute-done.42.high_ref = bf16[4,64,256]{2,1,0:T(8,128)(2,1)S(1)} collective-permute-done((bf16[4,64,256]{2,1,0:T(8,128)(2,1)S(1)}, bf16[4,64,256]{2,1,0:T(8,128)(2,1)S(1)}, u32[]{:S(2)}, u32[]{:S(2)}) %collective-permute-start.42) | collective-permute-done | bytes 131104 | tf_op jit(solution)/shard_map/ppermute | solution.py:191
  68.7 5.5 %collective-permute-done.41.low_ref = bf16[4,64,256]{2,1,0:T(8,128)(2,1)S(1)} collective-permute-done((bf16[4,64,256]{2,1,0:T(8,128)(2,1)S(1)}, bf16[4,64,256]{2,1,0:T(8,128)(2,1)S(1)}, u32[]{:S(2)}, u32[]{:S(2)}) %collective-permute-start.41) | collective-permute-done | bytes 131104 | tf_op jit(solution)/shard_map/ppermute | solution.py:191
  74.2 2.7 %shard_map.48 = f32[4,4,64,256]{3,2,1,0:T(8,128)} custom-call(f32[2]{0:T(128)S(1)} %add_convert_fusion.edge_ref, f32[4,4,64,256]{3,2,1,0:T(8,128)S(1)} %shard_map.47.q_ref, bf16[4,64,256]{2,1,0:T(8,128)(2,1)S(1)} %collective-permute-done.41.low_ref, bf16[4,64,256]{2,1,0:T(8,128)(2,1)S(1)} %collective-permute-done.42.high_ref, ...), custom_call_target="tpu_custom_call" | custom-call | flops 8000000 | bytes 4000000 | tf_op jit(solution)/shard_map/pallas_call | solution.py:171
  (13 shorter events, 0.4 us)
Async XLA Ops:
  2.4 5.9 %collective-permute-start.32 = (bf16[12,64,256]{2,1,0:T(8,128)(2,1)}, bf16[12,64,256]{2,1,0:T(8,128)(2,1)S(1)}, u32[]{:S(2)}, u32[]{:S(2)}) collective-permute-start(bf16[12,64,256]{2,1,0:T(8,128)(2,1)} %get-tuple-element.35), channel_id=1, source_target_pairs={{0,1},{1,0},{2,3},{3,2},{4,5},{5,4},{6,7},{7,6},{8,9},{9,8},{10,11... | collective-permute-start | bytes 1179656 | tf_op jit(solution)/shard_map/ppermute | solution.py:36
  9.4 0.9 %copy-start.2 = (bf16[4,64,256]{2,1,0:T(8,128)(2,1)S(1)}, bf16[4,64,256]{2,1,0:T(8,128)(2,1)}, u32[]{:S(2)}) copy-start(bf16[4,64,256]{2,1,0:T(8,128)(2,1)} %get-tuple-element.36) | copy-start | bytes 393220
  9.4 2.1 %copy-start.1 = (bf16[4,64,256]{2,1,0:T(8,128)(2,1)S(1)}, bf16[4,64,256]{2,1,0:T(8,128)(2,1)}, u32[]{:S(2)}) copy-start(bf16[4,64,256]{2,1,0:T(8,128)(2,1)} %get-tuple-element.37) | copy-start | bytes 393220
  9.5 6.7 %collective-permute-start.36 = (bf16[6,64,256]{2,1,0:T(8,128)(2,1)S(1)}, bf16[6,64,256]{2,1,0:T(8,128)(2,1)S(1)}, u32[]{:S(2)}, u32[]{:S(2)}) collective-permute-start(bf16[6,64,256]{2,1,0:T(8,128)(2,1)S(1)} %dynamic-slice_bitcast_fusion), channel_id=1, source_target_pairs={{0,2},{1,3},{2,0},{3,1},{4,6},{5,7},{6,4},{7,5},{8,10},{9,11},{10,... | collective-permute-start | bytes 589832 | tf_op jit(solution)/shard_map/ppermute | solution.py:36
  10.3 22.0 %collective-permute-start.34 = (bf16[4,64,256]{2,1,0:T(8,128)(2,1)S(1)}, bf16[4,64,256]{2,1,0:T(8,128)(2,1)S(1)}, u32[]{:S(2)}, u32[]{:S(2)}) collective-permute-start(bf16[4,64,256]{2,1,0:T(8,128)(2,1)S(1)} %copy-done.2), channel_id=1, source_target_pairs={{0,32},{32,64},{64,96},{96,128},{128,160},{160,192},{192,224},{224... | collective-permute-start | bytes 393224 | tf_op jit(solution)/shard_map/ppermute | solution.py:191
  11.5 20.9 %collective-permute-start.35 = (bf16[4,64,256]{2,1,0:T(8,128)(2,1)S(1)}, bf16[4,64,256]{2,1,0:T(8,128)(2,1)S(1)}, u32[]{:S(2)}, u32[]{:S(2)}) collective-permute-start(bf16[4,64,256]{2,1,0:T(8,128)(2,1)S(1)} %copy-done.1), channel_id=1, source_target_pairs={{32,0},{64,32},{96,64},{128,96},{160,128},{192,160},{224,192},{0,2... | collective-permute-start | bytes 393224 | tf_op jit(solution)/shard_map/ppermute | solution.py:191
  15.4 16.9 %collective-permute-start.33 = (bf16[6,64,256]{2,1,0:T(8,128)(2,1)S(1)}, bf16[6,64,256]{2,1,0:T(8,128)(2,1)S(1)}, u32[]{:S(2)}, u32[]{:S(2)}) collective-permute-start(bf16[6,64,256]{2,1,0:T(8,128)(2,1)S(1)} %dynamic-slice_bitcast_fusion.1), channel_id=1, source_target_pairs={{0,2},{1,3},{2,0},{3,1},{4,6},{5,7},{6,4},{7,5},{8,10},{9,11},{10,... | collective-permute-start | bytes 589832 | tf_op jit(solution)/shard_map/ppermute | solution.py:36
  16.3 2.7 %collective-permute-start.9 = (bf16[6,64,256]{2,1,0:T(8,128)(2,1)S(1)}, bf16[6,64,256]{2,1,0:T(8,128)(2,1)}, u32[]{:S(2)}, u32[]{:S(2)}) collective-permute-start(bf16[6,64,256]{2,1,0:T(8,128)(2,1)S(1)} %param.4), channel_id=1, source_target_pairs={{16,4},{17,5},{18,6},{19,7},{48,36},{49,37},{50,38},{51,39},{80,68... | collective-permute-start | bytes 589832 | tf_op jit(solution)/shard_map/cond/branch_4_fun/ppermute | solution.py:36
  17.6 1.3 %collective-permute-start.8 = (bf16[6,64,256]{2,1,0:T(8,128)(2,1)S(1)}, bf16[6,64,256]{2,1,0:T(8,128)(2,1)}, u32[]{:S(2)}, u32[]{:S(2)}) collective-permute-start(bf16[6,64,256]{2,1,0:T(8,128)(2,1)S(1)} %param.4), channel_id=1, source_target_pairs={{16,28},{17,29},{18,30},{19,31},{48,60},{49,61},{50,62},{51,63},{8... | collective-permute-start | bytes 589832 | tf_op jit(solution)/shard_map/cond/branch_4_fun/ppermute | solution.py:36
  19.0 24.1 %collective-permute-start.38 = (bf16[6,64,256]{2,1,0:T(8,128)(2,1)S(1)}, bf16[6,64,256]{2,1,0:T(8,128)(2,1)S(1)}, u32[]{:S(2)}, u32[]{:S(2)}) collective-permute-start(bf16[6,64,256]{2,1,0:T(8,128)(2,1)S(1)} %select_select_fusion.3), channel_id=1, source_target_pairs={{0,28},{1,29},{2,30},{3,31},{4,0},{5,1},{6,2},{7,3},{8,4},{9,5},{1... | collective-permute-start | bytes 589832 | tf_op jit(solution)/shard_map/ppermute | solution.py:36
  32.3 10.8 %collective-permute-start.37 = (bf16[6,64,256]{2,1,0:T(8,128)(2,1)S(1)}, bf16[6,64,256]{2,1,0:T(8,128)(2,1)S(1)}, u32[]{:S(2)}, u32[]{:S(2)}) collective-permute-start(bf16[6,64,256]{2,1,0:T(8,128)(2,1)S(1)} %select_select_fusion.3), channel_id=1, source_target_pairs={{0,4},{1,5},{2,6},{3,7},{4,8},{5,9},{6,10},{7,11},{8,12},{9,13},{1... | collective-permute-start | bytes 589832 | tf_op jit(solution)/shard_map/ppermute | solution.py:36
  32.4 2.7 %collective-permute-start.31 = (bf16[6,64,256]{2,1,0:T(8,128)(2,1)S(1)}, bf16[6,64,256]{2,1,0:T(8,128)(2,1)}, u32[]{:S(2)}, u32[]{:S(2)}) collective-permute-start(bf16[6,64,256]{2,1,0:T(8,128)(2,1)S(1)} %param.15), channel_id=1, source_target_pairs={{28,16},{29,17},{30,18},{31,19},{60,48},{61,49},{62,50},{63,51},{9... | collective-permute-start | bytes 589832 | tf_op jit(solution)/shard_map/cond/branch_7_fun/ppermute | solution.py:36
  33.7 1.3 %collective-permute-start.30 = (bf16[6,64,256]{2,1,0:T(8,128)(2,1)S(1)}, bf16[6,64,256]{2,1,0:T(8,128)(2,1)}, u32[]{:S(2)}, u32[]{:S(2)}) collective-permute-start(bf16[6,64,256]{2,1,0:T(8,128)(2,1)S(1)} %param.15), channel_id=1, source_target_pairs={{28,8},{29,9},{30,10},{31,11},{60,40},{61,41},{62,42},{63,43},{92,... | collective-permute-start | bytes 589832 | tf_op jit(solution)/shard_map/cond/branch_7_fun/ppermute | solution.py:36
  35.1 10.6 %collective-permute-start.44 = (bf16[6,64,256]{2,1,0:T(8,128)(2,1)S(1)}, bf16[6,64,256]{2,1,0:T(8,128)(2,1)S(1)}, u32[]{:S(2)}, u32[]{:S(2)}) collective-permute-start(bf16[6,64,256]{2,1,0:T(8,128)(2,1)S(1)} %select_select_fusion.1), channel_id=1, source_target_pairs={{0,28},{1,29},{2,30},{3,31},{4,0},{5,1},{6,2},{7,3},{8,4},{9,5},{1... | collective-permute-start | bytes 589832 | tf_op jit(solution)/shard_map/ppermute | solution.py:36
  43.1 5.7 %collective-permute-start.43 = (bf16[6,64,256]{2,1,0:T(8,128)(2,1)S(1)}, bf16[6,64,256]{2,1,0:T(8,128)(2,1)S(1)}, u32[]{:S(2)}, u32[]{:S(2)}) collective-permute-start(bf16[6,64,256]{2,1,0:T(8,128)(2,1)S(1)} %select_select_fusion.1), channel_id=1, source_target_pairs={{0,4},{1,5},{2,6},{3,7},{4,8},{5,9},{6,10},{7,11},{8,12},{9,13},{1... | collective-permute-start | bytes 589832 | tf_op jit(solution)/shard_map/ppermute | solution.py:36
  43.2 6.2 %collective-permute-start.39 = (bf16[6,64,256]{2,1,0:T(8,128)(2,1)S(1)}, bf16[6,64,256]{2,1,0:T(8,128)(2,1)S(1)}, u32[]{:S(2)}, u32[]{:S(2)}) collective-permute-start(bf16[6,64,256]{2,1,0:T(8,128)(2,1)S(1)} %select_select_fusion.2), channel_id=1, source_target_pairs={{0,2},{1,3},{2,0},{3,1},{4,6},{5,7},{6,4},{7,5},{8,10},{9,11},{10,... | collective-permute-start | bytes 589832 | tf_op jit(solution)/shard_map/ppermute | solution.py:36
  48.9 4.6 %collective-permute-start.45 = (bf16[6,64,256]{2,1,0:T(8,128)(2,1)S(1)}, bf16[6,64,256]{2,1,0:T(8,128)(2,1)S(1)}, u32[]{:S(2)}, u32[]{:S(2)}) collective-permute-start(bf16[6,64,256]{2,1,0:T(8,128)(2,1)S(1)} %select_select_fusion), channel_id=1, source_target_pairs={{0,2},{1,3},{2,0},{3,1},{4,6},{5,7},{6,4},{7,5},{8,10},{9,11},{10,... | collective-permute-start | bytes 589832 | tf_op jit(solution)/shard_map/ppermute | solution.py:36
  49.4 8.8 %collective-permute-start.40 = (bf16[12,64,256]{2,1,0:T(8,128)(2,1)S(1)}, bf16[12,64,256]{2,1,0:T(8,128)(2,1)S(1)}, u32[]{:S(2)}, u32[]{:S(2)}) collective-permute-start(bf16[12,64,256]{2,1,0:T(8,128)(2,1)S(1)} %pad_maximum_fusion.2), channel_id=1, source_target_pairs={{0,1},{1,0},{2,3},{3,2},{4,5},{5,4},{6,7},{7,6},{8,9},{9,8},{10,11... | collective-permute-start | bytes 1179656 | tf_op jit(solution)/shard_map/ppermute | solution.py:36
  53.6 12.2 %collective-permute-start.46 = (bf16[12,64,256]{2,1,0:T(8,128)(2,1)S(1)}, bf16[12,64,256]{2,1,0:T(8,128)(2,1)S(1)}, u32[]{:S(2)}, u32[]{:S(2)}) collective-permute-start(bf16[12,64,256]{2,1,0:T(8,128)(2,1)S(1)} %pad_maximum_fusion.3), channel_id=1, source_target_pairs={{0,1},{1,0},{2,3},{3,2},{4,5},{5,4},{6,7},{7,6},{8,9},{9,8},{10,11... | collective-permute-start | bytes 1179656 | tf_op jit(solution)/shard_map/ppermute | solution.py:36
  58.3 1.2 %copy-start = (f32[1,4,4,64,256]{4,3,2,1,0:T(8,128)S(1)}, f32[1,4,4,64,256]{4,3,2,1,0:T(8,128)}, u32[]{:S(2)}) copy-start(f32[1,4,4,64,256]{4,3,2,1,0:T(8,128)} %fields_hbm.1) | copy-start | bytes 3145732
  61.1 7.5 %collective-permute-start.42 = (bf16[4,64,256]{2,1,0:T(8,128)(2,1)S(1)}, bf16[4,64,256]{2,1,0:T(8,128)(2,1)S(1)}, u32[]{:S(2)}, u32[]{:S(2)}) collective-permute-start(bf16[4,64,256]{2,1,0:T(8,128)(2,1)S(1)} %get-tuple-element.51), channel_id=1, source_target_pairs={{32,0},{64,32},{96,64},{128,96},{160,128},{192,160},{224,192},{0,2... | collective-permute-start | bytes 393224 | tf_op jit(solution)/shard_map/ppermute | solution.py:191
  65.8 8.4 %collective-permute-start.41 = (bf16[4,64,256]{2,1,0:T(8,128)(2,1)S(1)}, bf16[4,64,256]{2,1,0:T(8,128)(2,1)S(1)}, u32[]{:S(2)}, u32[]{:S(2)}) collective-permute-start(bf16[4,64,256]{2,1,0:T(8,128)(2,1)S(1)} %get-tuple-element.52), channel_id=1, source_target_pairs={{0,32},{32,64},{64,96},{96,128},{128,160},{160,192},{192,224},{224... | collective-permute-start | bytes 393224 | tf_op jit(solution)/shard_map/ppermute | solution.py:191
where the time goes:
time: 78 us; the launch traced here: 76.8 us
  starting transfers between devices  50.1 us (64%)
  waiting for transfers between devices  13.6 us (17%)
  Pallas kernels  6.66 us (9%)
  between operations  2.81 us (4%)
  local copies, waits for them, and re-layouts  1.97 us (3%)
  other arithmetic  1.7 us (2%)
    ppermute x15, starting transfers between devices, move(): return lax.ppermute(value, 'group', pattern)  40.3 us
    ppermute x2, starting transfers between devices, ring_halo(): lax.ppermute(first, 'space', backward)  8.56 us
    ppermute x2, waiting for transfers between devices, ring_halo(): lax.ppermute(last, 'space', forward)  5.49 us
    ppermute x15, waiting for transfers between devices, move(): return lax.ppermute(value, 'group', pattern)  5.32 us
    pallas_call x2, Pallas kernels, advance(): pl.pallas_call(step_kernel, out_shape=jax.ShapeDtypeStruct(fields.shape,...  4.27 us
    ppermute x2, waiting for transfers between devices, ring_halo(): lax.ppermute(first, 'space', backward)  2.76 us
    pallas_call x1, Pallas kernels, decode_slice(): pl.pallas_call(decode_kernel, out_shape=(half, half, edge, edge, jax.Shap...  2.4 us
    unnamed x6, local copies, waits for them, and re-layouts  1.9 us
  transfers between devices with their start and end apart: 19, of which 4 were waited for; matrix products, arithmetic and copies ran while one was open for 1% of the time, Pallas kernels for 2%

commit v1 on v0

v1 whole, which is shorter than its diff:
```python
import jax
import jax.numpy as jnp
from jax import lax
from jax.experimental import pallas as pl
from jax.experimental.pallas import tpu as pltpu
from jax.sharding import PartitionSpec as P

STEPS = 2

SATURATION_SLOPE = 2.0
SHARPNESS = 4.0
CONDENSE_RATE = 0.25
LATENT_HEAT = 0.3

GROUP = 32
RING = 8
SPACE = 8
PLANES, LEVELS, WIDTH = 4, 64, 256
BLOCK = 16
MIB = 1024 * 1024

VMEM = pl.BlockSpec(memory_space=pltpu.VMEM)
SMEM = pl.BlockSpec(memory_space=pltpu.SMEM)
HBM = pl.BlockSpec(memory_space=pltpu.HBM)


def spot(z, x, c):
    return (z % RING) * 4 + x * 2 + c


def shift_pattern(step, planes=range(RING)):
    return [
        (spot(z, x, c), spot(z + step, x, c)) for z in planes for x in range(2) for c in range(2)
    ]


X_PATTERN = [(i, i ^ 2) for i in range(GROUP)]
C_PATTERN = [(i, i ^ 1) for i in range(GROUP)]
FORWARD = [(i, (i + 1) % SPACE) for i in range(SPACE)]
BACKWARD = [(target, source) for source, target in FORWARD]


def move(value, pattern):
    return lax.ppermute(value, "group", pattern)


def pick(flag, yes, no):
    return jnp.where(flag, yes, no)


def decode_kernel(
    stored_hbm, table_hbm, steps_hbm, fields_hbm,
    keep_ref, send_ref, bottom_ref, top_ref, owner_ref,
    stored_ref, table_ref, steps_ref, edge_ref, sems,
):
    small = [
        pltpu.make_async_copy(table_hbm, table_ref, sems.at[4]),
        pltpu.make_async_copy(steps_hbm, steps_ref, sems.at[5]),
    ]
    copies = [
        pltpu.make_async_copy(stored_hbm.at[0, :, p], stored_ref.at[p], sems.at[p])
        for p in range(PLANES)
    ]
    sides = [
        pltpu.make_async_copy(fields_hbm.at[0, :, 3 * k], edge_ref.at[k], sems.at[6 + k])
        for k in range(2)
    ]
    for copy in small + copies + sides:
        copy.start()
    mine = lax.rem(lax.axis_index("group"), 2)
    for p in range(PLANES):
        copies[p].wait()
        values = []
        for start in range(0, LEVELS, 32):
            rows = slice(start, start + 32)
            potential, exner_value, moisture, density = (
                1.0 + scale * stored_ref[p, k, rows, :].astype(jnp.float32)
                for k, scale in ((4, 0.4), (5, 0.4), (6, 2.0), (7, 0.8))
            )
            saturated = jnp.exp(SATURATION_SLOPE * (potential * exner_value - 1.0)) / density
            weight = jax.nn.sigmoid(SHARPNESS * (moisture - saturated))
            uptake = weight.astype(jnp.bfloat16)
            coupling = (weight * SATURATION_SLOPE * exner_value * saturated).astype(jnp.bfloat16)
            stored_ref[p, 4, rows, :] = uptake
            stored_ref[p, 5, rows, :] = coupling

        @pl.when(mine == p // 2)
        def _():
            keep_ref[p % 2] = stored_ref[p, 0:6]

        @pl.when(mine != p // 2)
        def _():
            send_ref[p % 2] = stored_ref[p, 0:6]

    for k, target in enumerate((bottom_ref, top_ref)):
        sides[k].wait()
        target[...] = edge_ref[k].astype(jnp.bfloat16)
    for copy in small:
        copy.wait()
    owner_ref[0] = table_ref[steps_ref[0]] + GROUP * table_ref[steps_ref[1]]


def decode_slice(trajectory, slot_table, step_indices, perturbations):
    half = jax.ShapeDtypeStruct((2, 6, LEVELS, WIDTH), jnp.bfloat16)
    edge = jax.ShapeDtypeStruct((4, LEVELS, WIDTH), jnp.bfloat16)
    return pl.pallas_call(
        decode_kernel,
        out_shape=(half, half, edge, edge, jax.ShapeDtypeStruct((1,), jnp.int32)),
        in_specs=[HBM] * 4,
        out_specs=(VMEM, VMEM, VMEM, VMEM, SMEM),
        scratch_shapes=[
            pltpu.VMEM((PLANES, 8, LEVELS, WIDTH), jnp.bfloat16),
            pltpu.SMEM((GROUP,), jnp.int32),
            pltpu.SMEM((STEPS,), jnp.int32),
            pltpu.VMEM((2, 4, LEVELS, WIDTH), jnp.float32),
            pltpu.SemaphoreType.DMA((8,)),
        ],
        compiler_params=pltpu.CompilerParams(vmem_limit_bytes=56 * MIB),
        cost_estimate=pl.CostEstimate(
            flops=1_500_000, bytes_accessed=3_500_000, transcendentals=200_000
        ),
    )(trajectory, slot_table, step_indices, perturbations)


def stencil(coef, centre, west, east, out, west_on=None, east_on=None):
    column = lax.broadcasted_iota(jnp.int32, (BLOCK, WIDTH), 1)
    row = lax.broadcasted_iota(jnp.int32, (BLOCK, WIDTH), 0)
    for start in range(0, LEVELS, BLOCK):
        rows = slice(start, start + BLOCK)
        speed = [coef(k, rows).astype(jnp.float32) for k in range(6)]
        diffusion = 0.025 + 0.06 * speed[3]
        west_w = jnp.maximum(speed[0], 0.0) + diffusion
        east_w = diffusion - jnp.minimum(speed[0], 0.0)
        south_w = jnp.maximum(speed[1], 0.0) + diffusion
        north_w = diffusion - jnp.minimum(speed[1], 0.0)
        below_w = jnp.maximum(speed[2], 0.0) + diffusion
        above_w = diffusion - jnp.minimum(speed[2], 0.0)
        centre_w = 1.0 - (west_w + east_w + south_w + north_w + below_w + above_w)
        south_w = jnp.where(column == 0, 0.0, south_w)
        north_w = jnp.where(column == WIDTH - 1, 0.0, north_w)
        if start == 0:
            below_w = jnp.where(row == 0, 0.0, below_w)
        if start + BLOCK == LEVELS:
            above_w = jnp.where(row == BLOCK - 1, 0.0, above_w)
        if west_on is not None:
            west_w = west_w * west_on
        if east_on is not None:
            east_w = east_w * east_on
        carried = []
        for field in range(4):
            here = centre(field, rows)
            if start == 0:
                below = pltpu.roll(here, 1, 0)
            else:
                below = centre(field, slice(start - 1, start + BLOCK - 1))
            if start + BLOCK == LEVELS:
                above = pltpu.roll(here, BLOCK - 1, 0)
            else:
                above = centre(field, slice(start + 1, start + BLOCK + 1))
            carried.append(
                (centre_w * here + west_w * west(field, rows))
                + (east_w * east(field, rows) + south_w * pltpu.roll(here, 1, 1))
                + (north_w * pltpu.roll(here, WIDTH - 1, 1) + below_w * below)
                + above_w * above
            )
        condense = CONDENSE_RATE * (speed[4] * carried[1] - speed[5] * carried[0])
        out(0, rows, carried[0] + LATENT_HEAT * condense)
        out(1, rows, carried[1] - condense)
        out(2, rows, carried[2] + condense)
        out(3, rows, carried[3])


def reader(ref, plane):
    return lambda field, rows: ref[field, plane, rows, :].astype(jnp.float32)


def writer(ref, plane):
    def write(field, rows, value):
        ref[field, plane, rows, :] = value

    return write


def coefficient(ref, plane):
    return lambda k, rows: ref[plane, k, rows, :]


def edge_reader(ref):
    return lambda field, rows: ref[field, rows, :].astype(jnp.float32)


def slab(on_ref, q_ref, high_ref, low_ref, coef_ref, out_ref, done=lambda p: None):
    for p in range(PLANES):
        stencil(
            coefficient(coef_ref, p),
            reader(q_ref, p),
            reader(q_ref, p - 1) if p else edge_reader(low_ref),
            reader(q_ref, p + 1) if p + 1 < PLANES else edge_reader(high_ref),
            writer(out_ref, p),
            on_ref[0] if p == 0 else None,
            on_ref[1] if p + 1 == PLANES else None,
        )
        done(p)


def second_kernel(on_ref, q_ref, high_ref, low_ref, coef_ref, out_hbm, out_ref, sems):
    copies = [
        pltpu.make_async_copy(out_ref.at[:, p], out_hbm.at[:, p], sems.at[p])
        for p in range(PLANES)
    ]
    slab(on_ref, q_ref, high_ref, low_ref, coef_ref, out_ref, lambda p: copies[p].start())
    for copy in copies:
        copy.wait()


def step(kernel, out_spec, scratch, arrays):
    return pl.pallas_call(
        kernel,
        out_shape=jax.ShapeDtypeStruct((4, PLANES, LEVELS, WIDTH), jnp.float32),
        in_specs=[SMEM] + [VMEM] * 4,
        out_specs=out_spec,
        scratch_shapes=scratch,
        compiler_params=pltpu.CompilerParams(vmem_limit_bytes=24 * MIB),
        cost_estimate=pl.CostEstimate(
            flops=8_000_000, bytes_accessed=4_000_000, transcendentals=0
        ),
    )(*arrays)


def first_step(*arrays):
    return step(slab, VMEM, [], arrays)


def second_step(*arrays):
    scratch = [
        pltpu.VMEM((4, PLANES, LEVELS, WIDTH), jnp.float32),
        pltpu.SemaphoreType.DMA((PLANES,)),
    ]
    return step(second_kernel, HBM, scratch, arrays)


def far_branch(plane):
    def send(piece):
        return move(piece, shift_pattern(3, [plane])), move(piece, shift_pattern(-3, [plane]))

    return send


def far(piece, plane, distance):
    up, down = lax.switch(plane, [far_branch(p) for p in range(RING)], piece)
    return pick(distance == 3, up, pick(distance == 5, down, piece))


def near_moves(held):
    return move(held, shift_pattern(1)), move(held, shift_pattern(-1))


def near_pick(held, plus, minus, distance):
    keep = (distance == 0) | (distance == 3) | (distance == 5)
    from_low = (distance == 1) | (distance == 4) | (distance == 6)
    return pick(keep, held, pick(from_low, plus, minus))


def ordered(flag, own, got):
    return jnp.stack([pick(flag, got, own), pick(flag, own, got)])


def on_device(perturbations, trajectory, slot_table, step_indices):
    me = lax.axis_index("group")
    my_z, my_x, my_c = me // 4, (me // 2) % 2, me % 2
    space = lax.axis_index("space")
    on = jnp.stack([space > 0, space < SPACE - 1]).astype(jnp.float32)

    mine, sent, bottom, top, packed = decode_slice(
        trajectory, slot_table, step_indices, perturbations
    )
    other = move(sent, C_PATTERN)
    packed = packed[0]
    owners = [packed % GROUP, packed // GROUP]
    planes = [owner // 4 for owner in owners]
    distance = [(my_z - z) % RING for z in planes]
    low = lax.ppermute(top, "space", FORWARD)
    high = lax.ppermute(bottom, "space", BACKWARD)

    fields = perturbations[0]
    waiting = []
    for owner in owners:
        half = pick(owner % 2 == my_c, mine, other)
        keep = lax.dynamic_index_in_dim(half, my_x, 0, keepdims=False)
        got = move(lax.dynamic_index_in_dim(half, 1 - my_x, 0, keepdims=False), X_PATTERN)
        waiting.append((keep, got))
    pieces = [
        pick((owner // 2) % 2 == my_x, keep, got) for owner, (keep, got) in zip(owners, waiting)
    ]

    first = far(pieces[0], planes[0], distance[0])
    first_moves = near_moves(first)
    second, low, high = lax.optimization_barrier((pieces[1], low, high))
    second = far(second, planes[1], distance[1])
    second, first_moves = lax.optimization_barrier((second, first_moves))
    first = near_pick(first, *first_moves, distance[0])
    pair = ordered(my_x == 1, first, move(first, X_PATTERN))
    second = near_pick(second, *near_moves(second), distance[1])
    got, other = move(second, X_PATTERN), move(pair, C_PATTERN)
    whole = ordered(my_c == 1, pair, other).reshape(PLANES, 6, LEVELS, WIDTH)
    fields = first_step(on, fields, high, low, whole)
    got, _ = lax.optimization_barrier((got, fields))
    low = lax.ppermute(fields[:, -1].astype(jnp.bfloat16), "space", FORWARD)
    high = lax.ppermute(fields[:, 0].astype(jnp.bfloat16), "space", BACKWARD)
    pair = ordered(my_x == 1, second, got)
    whole = ordered(my_c == 1, pair, move(pair, C_PATTERN)).reshape(PLANES, 6, LEVELS, WIDTH)
    return second_step(on, fields, high, low, whole)[None]


def solution(mesh):
    return jax.shard_map(
        on_device,
        mesh=mesh,
        in_specs=(
            P("group", None, "space", None, None),
            P("group", None, "space", None, None),
            P(),
            P(),
        ),
        out_specs=P("group", None, "space", None, None),
        check_vma=False,
    )
```

time: 78 us -> 74 us (0.949)
  waiting for transfers between devices: 13.6 us -> 11.4 us
  starting transfers between devices: 50.1 us -> 49 us
    ppermute x4, waiting for transfers between devices: 8.26 us -> 5.06 us  [the longest x1 3.5 us: on_device(): low = lax.ppermute(fields[:, -1].astype(jnp.bfloat16), 'space', FORWARD)]
    ppermute x15, starting transfers between devices: 40.3 us -> 38.7 us  [move(): return lax.ppermute(value, 'group', pattern)]
    ppermute x15, waiting for transfers between devices: 5.32 us -> 6.37 us  [move(): return lax.ppermute(value, 'group', pattern)]
  transfers between devices with their start and end apart: 19 -> 19, of which waited for: 4 -> 8; matrix products, arithmetic and copies ran while one was open for 1% -> 1% of each run, Pallas kernels for 2% -> 2%
where the time goes in v1:
time: 74 us; the launch traced here: 73.5 us
  starting transfers between devices  49 us (66%)
  waiting for transfers between devices  11.4 us (15%)
  Pallas kernels  6.42 us (9%)
  between operations  2.95 us (4%)
  local copies, waits for them, and re-layouts  1.96 us (3%)
  other arithmetic  1.72 us (2%)
    ppermute x15, starting transfers between devices, move(): return lax.ppermute(value, 'group', pattern)  38.7 us
    ppermute x15, waiting for transfers between devices, move(): return lax.ppermute(value, 'group', pattern)  6.37 us
    pallas_call x2, Pallas kernels, step(): pl.pallas_call(kernel, out_shape=jax.ShapeDtypeStruct((4, PLANES, LEVELS,...  4.03 us
    ppermute x1, starting transfers between devices, on_device(): high = lax.ppermute(bottom, 'space', BACKWARD)  3.92 us
    ppermute x1, waiting for transfers between devices, on_device(): low = lax.ppermute(fields[:, -1].astype(jnp.bfloat16), 'space', FORWARD)  3.5 us
    ppermute x1, starting transfers between devices, on_device(): high = lax.ppermute(fields[:, 0].astype(jnp.bfloat16), 'space', BACKWARD)  2.78 us
    pallas_call x1, Pallas kernels, decode_slice(): pl.pallas_call(decode_kernel, out_shape=(half, half, edge, edge, jax.Shap...  2.4 us
    ppermute x1, starting transfers between devices, on_device(): low = lax.ppermute(fields[:, -1].astype(jnp.bfloat16), 'space', FORWARD)  2.37 us
  transfers between devices with their start and end apart: 19, of which 8 were waited for; matrix products, arithmetic and copies ran while one was open for 1% of the time, Pallas kernels for 2%

profile of v1, /device:TPU:1, one launch (start us, length us, event | category | flops | bytes accessed | tf_op | source)
XLA Modules:
  0.0 73.5 jit_solution(17097220985642709518)
XLA Ops:
  0.0 2.4 %shard_map.46 = (bf16[2,6,64,256]{3,2,1,0:T(8,128)(2,1)}, bf16[2,6,64,256]{3,2,1,0:T(8,128)(2,1)}, bf16[4,64,256]{2,1,0:T(8,128)(2,1)}, bf16[4,64,256]{2,1,0:T(8,128)(2,1)}, s32[1]{0:T(128)}) custom-call(bf16[1,8,4,64,256]{4,3,2,1,0:T(8,128)(2,1)} %stored_hbm.1, s32[32]{0:T(128)} %table_hbm.1, s32[2]{0:T(128)} %steps_hbm.1, f32[1,4,4,64,256]{4,3,2,1,0:T(8,128)} %fields_hbm.1), custom_call_target="tpu_custom_call" | custom-call | flops 1500000 | bytes 3500000 | tf_op jit(solution)/shard_map/pallas_call | solution.py:106
  2.4 3.3 %collective-permute-start.32 = (bf16[2,6,64,256]{3,2,1,0:T(8,128)(2,1)}, bf16[2,6,64,256]{3,2,1,0:T(8,128)(2,1)S(1)}, u32[]{:S(2)}, u32[]{:S(2)}) collective-permute-start(bf16[2,6,64,256]{3,2,1,0:T(8,128)(2,1)} %get-tuple-element.39), channel_id=1, source_target_pairs={{0,1},{1,0},{2,3},{3,2},{4,5},{5,4},{6,7},{7,6},{8,9},{9,8},{10,11... | collective-permute-start | bytes 1179656 | tf_op jit(solution)/shard_map/ppermute | solution.py:44
  8.3 0.0 collective-permute-done.32
  8.4 1.1 %broadcast_select_fusion = (bf16[2,6,64,256]{3,2,1,0:T(8,128)(2,1)S(1)}, bf16[2,6,64,256]{3,2,1,0:T(8,128)(2,1)S(1)}) fusion(bf16[2,6,64,256]{3,2,1,0:T(8,128)(2,1)} %get-tuple-element.38, bf16[2,6,64,256]{3,2,1,0:T(8,128)(2,1)S(1)} %collective-permute-done.32, pred[]{:T(512)S(6)} %eq.78, pred[]{:T(512)S(6)} %eq.71), kind=kLoop, calls=%fused_computation.9 | loop fusion | flops 393216 | bytes 1572866 | tf_op jit(solution)/shard_map/jit(_where)/select_n | solution.py:48
  9.4 0.0 copy-start.2
  9.4 0.0 copy-start.1
  9.5 0.1 collective-permute-start.36
  9.6 0.8 %copy-done.2 = bf16[4,64,256]{2,1,0:T(8,128)(2,1)S(1)} copy-done((bf16[4,64,256]{2,1,0:T(8,128)(2,1)S(1)}, bf16[4,64,256]{2,1,0:T(8,128)(2,1)}, u32[]{:S(2)}) %copy-start.2) | copy-done | bytes 131096
  10.3 1.2 %collective-permute-start.34 = (bf16[4,64,256]{2,1,0:T(8,128)(2,1)S(1)}, bf16[4,64,256]{2,1,0:T(8,128)(2,1)S(1)}, u32[]{:S(2)}, u32[]{:S(2)}) collective-permute-start(bf16[4,64,256]{2,1,0:T(8,128)(2,1)S(1)} %copy-done.2), channel_id=1, source_target_pairs={{0,32},{32,64},{64,96},{96,128},{128,160},{160,192},{192,224},{224... | collective-permute-start | bytes 393224 | tf_op jit(solution)/shard_map/ppermute | solution.py:282
  11.5 0.0 copy-done.1
  11.5 3.9 %collective-permute-start.35 = (bf16[4,64,256]{2,1,0:T(8,128)(2,1)S(1)}, bf16[4,64,256]{2,1,0:T(8,128)(2,1)S(1)}, u32[]{:S(2)}, u32[]{:S(2)}) collective-permute-start(bf16[4,64,256]{2,1,0:T(8,128)(2,1)S(1)} %copy-done.1), channel_id=1, source_target_pairs={{32,0},{64,32},{96,64},{128,96},{160,128},{192,160},{224,192},{0,2... | collective-permute-start | bytes 393224 | tf_op jit(solution)/shard_map/ppermute | solution.py:283
  15.4 0.8 %collective-permute-start.33 = (bf16[6,64,256]{2,1,0:T(8,128)(2,1)S(1)}, bf16[6,64,256]{2,1,0:T(8,128)(2,1)S(1)}, u32[]{:S(2)}, u32[]{:S(2)}) collective-permute-start(bf16[6,64,256]{2,1,0:T(8,128)(2,1)S(1)} %dynamic-slice_bitcast_fusion.1), channel_id=1, source_target_pairs={{0,2},{1,3},{2,0},{3,1},{4,6},{5,7},{6,4},{7,5},{8,10},{9,11},{10,... | collective-permute-start | bytes 589832 | tf_op jit(solution)/shard_map/ppermute | solution.py:44
  16.2 0.0 collective-permute-done.36
  16.2 12.5 %conditional.2 = (bf16[6,64,256]{2,1,0:T(8,128)(2,1)}, bf16[6,64,256]{2,1,0:T(8,128)(2,1)}) conditional(s32[]{:T(128)} %clamp.6, bf16[6,64,256]{2,1,0:T(8,128)(2,1)S(1)} %bitcast_select_fusion, bf16[6,64,256]{2,1,0:T(8,128)(2,1)S(1)} %bitcast_select_fusion, bf16[6,64,256]{2,1,0:T(8,128)(2,1)S(1)} %bitcast_select_fusion, ...), branch_computations={%region_0.1_spmd, %region_1.2_spmd, %region_2.3_spmd, %region_3.4_... | conditional | bytes 1572960 | solution.py:250
  16.3 7.8 %collective-permute-start.1 = (bf16[6,64,256]{2,1,0:T(8,128)(2,1)S(1)}, bf16[6,64,256]{2,1,0:T(8,128)(2,1)}, u32[]{:S(2)}, u32[]{:S(2)}) collective-permute-start(bf16[6,64,256]{2,1,0:T(8,128)(2,1)S(1)} %param), channel_id=1, source_target_pairs={{0,20},{1,21},{2,22},{3,23},{32,52},{33,53},{34,54},{35,55},{64,84... | collective-permute-start | bytes 589832 | tf_op jit(solution)/shard_map/cond/branch_0_fun/ppermute | solution.py:44
  24.1 2.0 %collective-permute-start = (bf16[6,64,256]{2,1,0:T(8,128)(2,1)S(1)}, bf16[6,64,256]{2,1,0:T(8,128)(2,1)}, u32[]{:S(2)}, u32[]{:S(2)}) collective-permute-start(bf16[6,64,256]{2,1,0:T(8,128)(2,1)S(1)} %param), channel_id=1, source_target_pairs={{0,12},{1,13},{2,14},{3,15},{32,44},{33,45},{34,46},{35,47},{64,76... | collective-permute-start | bytes 589832 | tf_op jit(solution)/shard_map/cond/branch_0_fun/ppermute | solution.py:44
  26.0 0.7 collective-permute-done.1
  26.8 1.9 %collective-permute-done = bf16[6,64,256]{2,1,0:T(8,128)(2,1)} collective-permute-done((bf16[6,64,256]{2,1,0:T(8,128)(2,1)S(1)}, bf16[6,64,256]{2,1,0:T(8,128)(2,1)}, u32[]{:S(2)}, u32[]{:S(2)}) %collective-permute-start) | collective-permute-done | bytes 196640 | tf_op jit(solution)/shard_map/cond/branch_0_fun/ppermute | solution.py:44
  28.7 0.1 collective-permute-start.38
  28.8 1.5 %collective-permute-start.37 = (bf16[6,64,256]{2,1,0:T(8,128)(2,1)S(1)}, bf16[6,64,256]{2,1,0:T(8,128)(2,1)S(1)}, u32[]{:S(2)}, u32[]{:S(2)}) collective-permute-start(bf16[6,64,256]{2,1,0:T(8,128)(2,1)S(1)} %select_select_fusion.3), channel_id=1, source_target_pairs={{0,4},{1,5},{2,6},{3,7},{4,8},{5,9},{6,10},{7,11},{8,12},{9,13},{1... | collective-permute-start | bytes 589832 | tf_op jit(solution)/shard_map/ppermute | solution.py:44
  30.3 0.0 collective-permute-done.33
  30.3 0.0 collective-permute-done.34.low_ref
  30.3 0.0 collective-permute-done.35.high_ref
  30.3 2.7 %conditional.3 = (bf16[6,64,256]{2,1,0:T(8,128)(2,1)}, bf16[6,64,256]{2,1,0:T(8,128)(2,1)}) conditional(s32[]{:T(128)} %clamp.7, bf16[6,64,256]{2,1,0:T(8,128)(2,1)S(1)} %bitcast_select_fusion.1, bf16[6,64,256]{2,1,0:T(8,128)(2,1)S(1)} %bitcast_select_fusion.1, ...), branch_computations={%region_8.9_spmd, %region_9.10_spmd, %region_10.11_spmd, %region_1... | conditional | bytes 1572960 | solution.py:250
  30.4 1.3 %collective-permute-start.31 = (bf16[6,64,256]{2,1,0:T(8,128)(2,1)S(1)}, bf16[6,64,256]{2,1,0:T(8,128)(2,1)}, u32[]{:S(2)}, u32[]{:S(2)}) collective-permute-start(bf16[6,64,256]{2,1,0:T(8,128)(2,1)S(1)} %param.15), channel_id=1, source_target_pairs={{28,16},{29,17},{30,18},{31,19},{60,48},{61,49},{62,50},{63,51},{9... | collective-permute-start | bytes 589832 | tf_op jit(solution)/shard_map/cond/branch_7_fun/ppermute | solution.py:44
  31.7 1.3 %collective-permute-start.30 = (bf16[6,64,256]{2,1,0:T(8,128)(2,1)S(1)}, bf16[6,64,256]{2,1,0:T(8,128)(2,1)}, u32[]{:S(2)}, u32[]{:S(2)}) collective-permute-start(bf16[6,64,256]{2,1,0:T(8,128)(2,1)S(1)} %param.15), channel_id=1, source_target_pairs={{28,8},{29,9},{30,10},{31,11},{60,40},{61,41},{62,42},{63,43},{92,... | collective-permute-start | bytes 589832 | tf_op jit(solution)/shard_map/cond/branch_7_fun/ppermute | solution.py:44
  33.0 0.0 collective-permute-done.31
  33.0 0.0 collective-permute-done.30
  33.1 0.2 collective-permute-done.38
  33.3 1.3 %collective-permute-done.37 = bf16[6,64,256]{2,1,0:T(8,128)(2,1)S(1)} collective-permute-done((bf16[6,64,256]{2,1,0:T(8,128)(2,1)S(1)}, bf16[6,64,256]{2,1,0:T(8,128)(2,1)S(1)}, u32[]{:S(2)}, u32[]{:S(2)}) %collective-permute-start.37) | collective-permute-done | bytes 196640 | tf_op jit(solution)/shard_map/ppermute | solution.py:44
  34.7 0.5 collective-permute-start.39
  35.1 8.5 %collective-permute-start.44 = (bf16[6,64,256]{2,1,0:T(8,128)(2,1)S(1)}, bf16[6,64,256]{2,1,0:T(8,128)(2,1)S(1)}, u32[]{:S(2)}, u32[]{:S(2)}) collective-permute-start(bf16[6,64,256]{2,1,0:T(8,128)(2,1)S(1)} %select_select_fusion.2), channel_id=1, source_target_pairs={{0,28},{1,29},{2,30},{3,31},{4,0},{5,1},{6,2},{7,3},{8,4},{9,5},{1... | collective-permute-start | bytes 589832 | tf_op jit(solution)/shard_map/ppermute | solution.py:44
  43.7 0.0 collective-permute-start.43
  43.7 0.0 collective-permute-done.39
  43.7 3.9 %collective-permute-start.40 = (bf16[2,6,64,256]{3,2,1,0:T(8,128)(2,1)S(1)}, bf16[2,6,64,256]{3,2,1,0:T(8,128)(2,1)S(1)}, u32[]{:S(2)}, u32[]{:S(2)}) collective-permute-start(bf16[2,6,64,256]{3,2,1,0:T(8,128)(2,1)S(1)} %pad_maximum_fusion.2), channel_id=1, source_target_pairs={{0,1},{1,0},{2,3},{3,2},{4,5},{5,4},{6,7},{7,6},{8,9},{9,8},{10,11... | collective-permute-start | bytes 1179656 | tf_op jit(solution)/shard_map/ppermute | solution.py:44
  47.7 0.1 add_convert_fusion.on_ref
  47.8 0.0 collective-permute-done.44
  47.8 1.6 %collective-permute-done.43 = bf16[6,64,256]{2,1,0:T(8,128)(2,1)S(1)} collective-permute-done((bf16[6,64,256]{2,1,0:T(8,128)(2,1)S(1)}, bf16[6,64,256]{2,1,0:T(8,128)(2,1)S(1)}, u32[]{:S(2)}, u32[]{:S(2)}) %collective-permute-start.43) | collective-permute-done | bytes 196640 | tf_op jit(solution)/shard_map/ppermute | solution.py:44
  49.4 1.3 %collective-permute-start.45 = (bf16[6,64,256]{2,1,0:T(8,128)(2,1)S(1)}, bf16[6,64,256]{2,1,0:T(8,128)(2,1)S(1)}, u32[]{:S(2)}, u32[]{:S(2)}) collective-permute-start(bf16[6,64,256]{2,1,0:T(8,128)(2,1)S(1)} %select_select_fusion), channel_id=1, source_target_pairs={{0,2},{1,3},{2,0},{3,1},{4,6},{5,7},{6,4},{7,5},{8,10},{9,11},{10,... | collective-permute-start | bytes 589832 | tf_op jit(solution)/shard_map/ppermute | solution.py:44
  50.8 0.0 collective-permute-done.40
  50.8 0.1 select_bitcast_fusion.3
  50.8 0.0 copy-start
  50.8 0.1 pad_maximum_fusion
  50.9 1.1 %copy-done = f32[1,4,4,64,256]{4,3,2,1,0:T(8,128)S(1)} copy-done((f32[1,4,4,64,256]{4,3,2,1,0:T(8,128)S(1)}, f32[1,4,4,64,256]{4,3,2,1,0:T(8,128)}, u32[]{:S(2)}) %copy-start) | copy-done | bytes 1048600
  52.0 1.6 %shard_map.47.q_ref = f32[4,4,64,256]{3,2,1,0:T(8,128)S(1)} custom-call(f32[2]{0:T(128)S(1)} %add_convert_fusion.on_ref, f32[4,4,64,256]{3,2,1,0:T(8,128)S(1)} %bitcast.35, bf16[4,64,256]{2,1,0:T(8,128)(2,1)S(1)} %collective-permute-done.35.high_ref, bf16[4,64,256]{2,1,0:T(8,128)(2,1)S(1)} %collective-permute-done.34.low_ref, ...), custom_call_target="tpu_custom_call" | custom-call | flops 8000000 | bytes 4000000 | tf_op jit(solution)/shard_map/pallas_call | solution.py:217
  53.7 0.5 collective-permute-done.45
  54.3 6.2 %collective-permute-start.46 = (bf16[2,6,64,256]{3,2,1,0:T(8,128)(2,1)S(1)}, bf16[2,6,64,256]{3,2,1,0:T(8,128)(2,1)S(1)}, u32[]{:S(2)}, u32[]{:S(2)}) collective-permute-start(bf16[2,6,64,256]{3,2,1,0:T(8,128)(2,1)S(1)} %pad_maximum_fusion.3), channel_id=1, source_target_pairs={{0,1},{1,0},{2,3},{3,2},{4,5},{5,4},{6,7},{7,6},{8,9},{9,8},{10,11... | collective-permute-start | bytes 1179656 | tf_op jit(solution)/shard_map/ppermute | solution.py:44
  60.6 2.4 %collective-permute-start.42 = (bf16[4,64,256]{2,1,0:T(8,128)(2,1)S(1)}, bf16[4,64,256]{2,1,0:T(8,128)(2,1)S(1)}, u32[]{:S(2)}, u32[]{:S(2)}) collective-permute-start(bf16[4,64,256]{2,1,0:T(8,128)(2,1)S(1)} %get-tuple-element.59), channel_id=1, source_target_pairs={{0,32},{32,64},{64,96},{96,128},{128,160},{160,192},{192,224},{224... | collective-permute-start | bytes 393224 | tf_op jit(solution)/shard_map/ppermute | solution.py:308
  63.0 2.8 %collective-permute-start.41 = (bf16[4,64,256]{2,1,0:T(8,128)(2,1)S(1)}, bf16[4,64,256]{2,1,0:T(8,128)(2,1)S(1)}, u32[]{:S(2)}, u32[]{:S(2)}) collective-permute-start(bf16[4,64,256]{2,1,0:T(8,128)(2,1)S(1)} %get-tuple-element.60), channel_id=1, source_target_pairs={{32,0},{64,32},{96,64},{128,96},{160,128},{192,160},{224,192},{0,2... | collective-permute-start | bytes 393224 | tf_op jit(solution)/shard_map/ppermute | solution.py:309
  65.7 0.0 collective-permute-done.46
  65.7 0.1 select_bitcast_fusion.1
  65.8 0.1 pad_maximum_fusion.1
  65.9 3.5 %collective-permute-done.42.low_ref = bf16[4,64,256]{2,1,0:T(8,128)(2,1)S(1)} collective-permute-done((bf16[4,64,256]{2,1,0:T(8,128)(2,1)S(1)}, bf16[4,64,256]{2,1,0:T(8,128)(2,1)S(1)}, u32[]{:S(2)}, u32[]{:S(2)}) %collective-permute-start.42) | collective-permute-done | bytes 131104 | tf_op jit(solution)/shard_map/ppermute | solution.py:308
  69.4 1.6 %collective-permute-done.41.high_ref = bf16[4,64,256]{2,1,0:T(8,128)(2,1)S(1)} collective-permute-done((bf16[4,64,256]{2,1,0:T(8,128)(2,1)S(1)}, bf16[4,64,256]{2,1,0:T(8,128)(2,1)S(1)}, u32[]{:S(2)}, u32[]{:S(2)}) %collective-permute-start.41) | collective-permute-done | bytes 131104 | tf_op jit(solution)/shard_map/ppermute | solution.py:309
  70.9 2.4 %shard_map.48 = f32[4,4,64,256]{3,2,1,0:T(8,128)} custom-call(f32[2]{0:T(128)S(1)} %add_convert_fusion.on_ref, f32[4,4,64,256]{3,2,1,0:T(8,128)S(1)} %shard_map.47.q_ref, bf16[4,64,256]{2,1,0:T(8,128)(2,1)S(1)} %collective-permute-done.41.high_ref, bf16[4,64,256]{2,1,0:T(8,128)(2,1)S(1)} %collective-permute-done.42.low_ref, bf16[4,6,64,256]{3,2,1,0:T(8,128)(2,1)S(1)} %bitcast.36), custom_call_target="tpu_custom_call" | custom-call | flops 8000000 | bytes 4000000 | tf_op jit(solution)/shard_map/pallas_call | solution.py:217
  (13 shorter events, 0.4 us)
Async XLA Ops:
  2.4 5.9 %collective-permute-start.32 = (bf16[2,6,64,256]{3,2,1,0:T(8,128)(2,1)}, bf16[2,6,64,256]{3,2,1,0:T(8,128)(2,1)S(1)}, u32[]{:S(2)}, u32[]{:S(2)}) collective-permute-start(bf16[2,6,64,256]{3,2,1,0:T(8,128)(2,1)} %get-tuple-element.39), channel_id=1, source_target_pairs={{0,1},{1,0},{2,3},{3,2},{4,5},{5,4},{6,7},{7,6},{8,9},{9,8},{10,11... | collective-permute-start | bytes 1179656 | tf_op jit(solution)/shard_map/ppermute | solution.py:44
  9.4 0.9 %copy-start.2 = (bf16[4,64,256]{2,1,0:T(8,128)(2,1)S(1)}, bf16[4,64,256]{2,1,0:T(8,128)(2,1)}, u32[]{:S(2)}) copy-start(bf16[4,64,256]{2,1,0:T(8,128)(2,1)} %get-tuple-element.40) | copy-start | bytes 393220
  9.4 2.1 %copy-start.1 = (bf16[4,64,256]{2,1,0:T(8,128)(2,1)S(1)}, bf16[4,64,256]{2,1,0:T(8,128)(2,1)}, u32[]{:S(2)}) copy-start(bf16[4,64,256]{2,1,0:T(8,128)(2,1)} %get-tuple-element.41) | copy-start | bytes 393220
  9.5 6.7 %collective-permute-start.36 = (bf16[6,64,256]{2,1,0:T(8,128)(2,1)S(1)}, bf16[6,64,256]{2,1,0:T(8,128)(2,1)S(1)}, u32[]{:S(2)}, u32[]{:S(2)}) collective-permute-start(bf16[6,64,256]{2,1,0:T(8,128)(2,1)S(1)} %dynamic-slice_bitcast_fusion), channel_id=1, source_target_pairs={{0,2},{1,3},{2,0},{3,1},{4,6},{5,7},{6,4},{7,5},{8,10},{9,11},{10,... | collective-permute-start | bytes 589832 | tf_op jit(solution)/shard_map/ppermute | solution.py:44
  10.3 20.0 %collective-permute-start.34 = (bf16[4,64,256]{2,1,0:T(8,128)(2,1)S(1)}, bf16[4,64,256]{2,1,0:T(8,128)(2,1)S(1)}, u32[]{:S(2)}, u32[]{:S(2)}) collective-permute-start(bf16[4,64,256]{2,1,0:T(8,128)(2,1)S(1)} %copy-done.2), channel_id=1, source_target_pairs={{0,32},{32,64},{64,96},{96,128},{128,160},{160,192},{192,224},{224... | collective-permute-start | bytes 393224 | tf_op jit(solution)/shard_map/ppermute | solution.py:282
  11.5 18.8 %collective-permute-start.35 = (bf16[4,64,256]{2,1,0:T(8,128)(2,1)S(1)}, bf16[4,64,256]{2,1,0:T(8,128)(2,1)S(1)}, u32[]{:S(2)}, u32[]{:S(2)}) collective-permute-start(bf16[4,64,256]{2,1,0:T(8,128)(2,1)S(1)} %copy-done.1), channel_id=1, source_target_pairs={{32,0},{64,32},{96,64},{128,96},{160,128},{192,160},{224,192},{0,2... | collective-permute-start | bytes 393224 | tf_op jit(solution)/shard_map/ppermute | solution.py:283
  15.4 14.9 %collective-permute-start.33 = (bf16[6,64,256]{2,1,0:T(8,128)(2,1)S(1)}, bf16[6,64,256]{2,1,0:T(8,128)(2,1)S(1)}, u32[]{:S(2)}, u32[]{:S(2)}) collective-permute-start(bf16[6,64,256]{2,1,0:T(8,128)(2,1)S(1)} %dynamic-slice_bitcast_fusion.1), channel_id=1, source_target_pairs={{0,2},{1,3},{2,0},{3,1},{4,6},{5,7},{6,4},{7,5},{8,10},{9,11},{10,... | collective-permute-start | bytes 589832 | tf_op jit(solution)/shard_map/ppermute | solution.py:44
  16.3 10.5 %collective-permute-start.1 = (bf16[6,64,256]{2,1,0:T(8,128)(2,1)S(1)}, bf16[6,64,256]{2,1,0:T(8,128)(2,1)}, u32[]{:S(2)}, u32[]{:S(2)}) collective-permute-start(bf16[6,64,256]{2,1,0:T(8,128)(2,1)S(1)} %param), channel_id=1, source_target_pairs={{0,20},{1,21},{2,22},{3,23},{32,52},{33,53},{34,54},{35,55},{64,84... | collective-permute-start | bytes 589832 | tf_op jit(solution)/shard_map/cond/branch_0_fun/ppermute | solution.py:44
  24.1 4.6 %collective-permute-start = (bf16[6,64,256]{2,1,0:T(8,128)(2,1)S(1)}, bf16[6,64,256]{2,1,0:T(8,128)(2,1)}, u32[]{:S(2)}, u32[]{:S(2)}) collective-permute-start(bf16[6,64,256]{2,1,0:T(8,128)(2,1)S(1)} %param), channel_id=1, source_target_pairs={{0,12},{1,13},{2,14},{3,15},{32,44},{33,45},{34,46},{35,47},{64,76... | collective-permute-start | bytes 589832 | tf_op jit(solution)/shard_map/cond/branch_0_fun/ppermute | solution.py:44
  28.7 4.6 %collective-permute-start.38 = (bf16[6,64,256]{2,1,0:T(8,128)(2,1)S(1)}, bf16[6,64,256]{2,1,0:T(8,128)(2,1)S(1)}, u32[]{:S(2)}, u32[]{:S(2)}) collective-permute-start(bf16[6,64,256]{2,1,0:T(8,128)(2,1)S(1)} %select_select_fusion.3), channel_id=1, source_target_pairs={{0,28},{1,29},{2,30},{3,31},{4,0},{5,1},{6,2},{7,3},{8,4},{9,5},{1... | collective-permute-start | bytes 589832 | tf_op jit(solution)/shard_map/ppermute | solution.py:44
  28.8 5.8 %collective-permute-start.37 = (bf16[6,64,256]{2,1,0:T(8,128)(2,1)S(1)}, bf16[6,64,256]{2,1,0:T(8,128)(2,1)S(1)}, u32[]{:S(2)}, u32[]{:S(2)}) collective-permute-start(bf16[6,64,256]{2,1,0:T(8,128)(2,1)S(1)} %select_select_fusion.3), channel_id=1, source_target_pairs={{0,4},{1,5},{2,6},{3,7},{4,8},{5,9},{6,10},{7,11},{8,12},{9,13},{1... | collective-permute-start | bytes 589832 | tf_op jit(solution)/shard_map/ppermute | solution.py:44
  30.4 2.7 %collective-permute-start.31 = (bf16[6,64,256]{2,1,0:T(8,128)(2,1)S(1)}, bf16[6,64,256]{2,1,0:T(8,128)(2,1)}, u32[]{:S(2)}, u32[]{:S(2)}) collective-permute-start(bf16[6,64,256]{2,1,0:T(8,128)(2,1)S(1)} %param.15), channel_id=1, source_target_pairs={{28,16},{29,17},{30,18},{31,19},{60,48},{61,49},{62,50},{63,51},{9... | collective-permute-start | bytes 589832 | tf_op jit(solution)/shard_map/cond/branch_7_fun/ppermute | solution.py:44
  31.7 1.3 %collective-permute-start.30 = (bf16[6,64,256]{2,1,0:T(8,128)(2,1)S(1)}, bf16[6,64,256]{2,1,0:T(8,128)(2,1)}, u32[]{:S(2)}, u32[]{:S(2)}) collective-permute-start(bf16[6,64,256]{2,1,0:T(8,128)(2,1)S(1)} %param.15), channel_id=1, source_target_pairs={{28,8},{29,9},{30,10},{31,11},{60,40},{61,41},{62,42},{63,43},{92,... | collective-permute-start | bytes 589832 | tf_op jit(solution)/shard_map/cond/branch_7_fun/ppermute | solution.py:44
  34.7 9.0 %collective-permute-start.39 = (bf16[6,64,256]{2,1,0:T(8,128)(2,1)S(1)}, bf16[6,64,256]{2,1,0:T(8,128)(2,1)S(1)}, u32[]{:S(2)}, u32[]{:S(2)}) collective-permute-start(bf16[6,64,256]{2,1,0:T(8,128)(2,1)S(1)} %select_select_fusion.1), channel_id=1, source_target_pairs={{0,2},{1,3},{2,0},{3,1},{4,6},{5,7},{6,4},{7,5},{8,10},{9,11},{10,... | collective-permute-start | bytes 589832 | tf_op jit(solution)/shard_map/ppermute | solution.py:44
  35.1 12.6 %collective-permute-start.44 = (bf16[6,64,256]{2,1,0:T(8,128)(2,1)S(1)}, bf16[6,64,256]{2,1,0:T(8,128)(2,1)S(1)}, u32[]{:S(2)}, u32[]{:S(2)}) collective-permute-start(bf16[6,64,256]{2,1,0:T(8,128)(2,1)S(1)} %select_select_fusion.2), channel_id=1, source_target_pairs={{0,28},{1,29},{2,30},{3,31},{4,0},{5,1},{6,2},{7,3},{8,4},{9,5},{1... | collective-permute-start | bytes 589832 | tf_op jit(solution)/shard_map/ppermute | solution.py:44
  43.7 5.7 %collective-permute-start.43 = (bf16[6,64,256]{2,1,0:T(8,128)(2,1)S(1)}, bf16[6,64,256]{2,1,0:T(8,128)(2,1)S(1)}, u32[]{:S(2)}, u32[]{:S(2)}) collective-permute-start(bf16[6,64,256]{2,1,0:T(8,128)(2,1)S(1)} %select_select_fusion.2), channel_id=1, source_target_pairs={{0,4},{1,5},{2,6},{3,7},{4,8},{5,9},{6,10},{7,11},{8,12},{9,13},{1... | collective-permute-start | bytes 589832 | tf_op jit(solution)/shard_map/ppermute | solution.py:44
  43.7 7.0 %collective-permute-start.40 = (bf16[2,6,64,256]{3,2,1,0:T(8,128)(2,1)S(1)}, bf16[2,6,64,256]{3,2,1,0:T(8,128)(2,1)S(1)}, u32[]{:S(2)}, u32[]{:S(2)}) collective-permute-start(bf16[2,6,64,256]{3,2,1,0:T(8,128)(2,1)S(1)} %pad_maximum_fusion.2), channel_id=1, source_target_pairs={{0,1},{1,0},{2,3},{3,2},{4,5},{5,4},{6,7},{7,6},{8,9},{9,8},{10,11... | collective-permute-start | bytes 1179656 | tf_op jit(solution)/shard_map/ppermute | solution.py:44
  49.4 4.8 %collective-permute-start.45 = (bf16[6,64,256]{2,1,0:T(8,128)(2,1)S(1)}, bf16[6,64,256]{2,1,0:T(8,128)(2,1)S(1)}, u32[]{:S(2)}, u32[]{:S(2)}) collective-permute-start(bf16[6,64,256]{2,1,0:T(8,128)(2,1)S(1)} %select_select_fusion), channel_id=1, source_target_pairs={{0,2},{1,3},{2,0},{3,1},{4,6},{5,7},{6,4},{7,5},{8,10},{9,11},{10,... | collective-permute-start | bytes 589832 | tf_op jit(solution)/shard_map/ppermute | solution.py:44
  50.8 1.2 %copy-start = (f32[1,4,4,64,256]{4,3,2,1,0:T(8,128)S(1)}, f32[1,4,4,64,256]{4,3,2,1,0:T(8,128)}, u32[]{:S(2)}) copy-start(f32[1,4,4,64,256]{4,3,2,1,0:T(8,128)} %fields_hbm.1) | copy-start | bytes 3145732
  54.3 11.4 %collective-permute-start.46 = (bf16[2,6,64,256]{3,2,1,0:T(8,128)(2,1)S(1)}, bf16[2,6,64,256]{3,2,1,0:T(8,128)(2,1)S(1)}, u32[]{:S(2)}, u32[]{:S(2)}) collective-permute-start(bf16[2,6,64,256]{3,2,1,0:T(8,128)(2,1)S(1)} %pad_maximum_fusion.3), channel_id=1, source_target_pairs={{0,1},{1,0},{2,3},{3,2},{4,5},{5,4},{6,7},{7,6},{8,9},{9,8},{10,11... | collective-permute-start | bytes 1179656 | tf_op jit(solution)/shard_map/ppermute | solution.py:44
  60.6 8.8 %collective-permute-start.42 = (bf16[4,64,256]{2,1,0:T(8,128)(2,1)S(1)}, bf16[4,64,256]{2,1,0:T(8,128)(2,1)S(1)}, u32[]{:S(2)}, u32[]{:S(2)}) collective-permute-start(bf16[4,64,256]{2,1,0:T(8,128)(2,1)S(1)} %get-tuple-element.59), channel_id=1, source_target_pairs={{0,32},{32,64},{64,96},{96,128},{128,160},{160,192},{192,224},{224... | collective-permute-start | bytes 393224 | tf_op jit(solution)/shard_map/ppermute | solution.py:308
  63.0 8.0 %collective-permute-start.41 = (bf16[4,64,256]{2,1,0:T(8,128)(2,1)S(1)}, bf16[4,64,256]{2,1,0:T(8,128)(2,1)S(1)}, u32[]{:S(2)}, u32[]{:S(2)}) collective-permute-start(bf16[4,64,256]{2,1,0:T(8,128)(2,1)S(1)} %get-tuple-element.60), channel_id=1, source_target_pairs={{32,0},{64,32},{96,64},{128,96},{160,128},{192,160},{224,192},{0,2... | collective-permute-start | bytes 393224 | tf_op jit(solution)/shard_map/ppermute | solution.py:309
